TPU v7x, 32 devices: a whole 2x2x4 slice. The times are simulated.
32 devices in a mesh: tile: 4 (over y, x), box: 4 (over z), slab: 2 (over core).
Axes of the slice: x: 2, y: 2, z: 4, core: 2. Of those that a mesh axis runs over, the one named last changes fastest.
Arguments:
- les: bfloat16 [1024, 3, 48, 256], P(('tile', 'box'), None, 'slab'), may hold values from -6 to 6
- tile_owner: int32 [80, 25, 1], replicated, may hold values from 0 to 15; in each aligned block of 125 rows (0 to 124, 125 to 249, ..., all dimensions but the last counted through in order) at most 9 rows name the same one
- tile_slot: int32 [80, 25], replicated, may hold values from 0 to 63
- box_offset: int32 [80, 2], P(('tile', 'box')), may hold values from 0 to 127
- plane_deficit: float32 [64, 64, 64], P(('tile', 'box'), 'slab'), may hold values from -2.4 to 2.4
- plane_box: int32 [64, 4], P(('tile', 'box')), may hold values from 0 to 79, as said below
- plane_weight: float32 [64, 4], P(('tile', 'box')), may hold values from 0.5 to 1.5
Outputs:
- inflow: bfloat16 [80, 3, 64, 4096], P(('tile', 'box'), None, 'slab')
Inputs may be any that keep to these rules, and one draw needn't show every extreme that they name: tile_owner[b, q, 0] is the device along tile+box that holds patch tile q of box b; over the 125 rows of the boxes of one owner no device is named more than 9 times. `plane_box`: box b belongs to owner b // 5; the 4 boxes of one plane have different owners, and over the planes held by one index of tile+box no owner is named more than 1 times, some owner exactly 1 times.
All inputs are finite; a program needn't handle non-finite values.
Results may differ from a plain program's by a relative error of at most 0.0039.
Values may be sent and summed in bfloat16 or wider, within the bound.
A program may use at most 128 MiB of HBM per device.

v0:
```python
import jax
import jax.numpy as jnp
from jax import lax
from jax.sharding import PartitionSpec as P

BOXN = 64
TS = 16
LZ = 48
FILTER_NU = 0.125


def padded(x, sides, width):
    for axis, dim in sides:
        size, length = (lax.axis_size(axis), x.shape[dim])
        up = [(i, (i + 1) % size) for i in range(size - 1)]
        down = [(j, i) for i, j in up]
        last = lax.slice_in_dim(x, length - width, length, axis=dim)
        initial = lax.slice_in_dim(x, 0, width, axis=dim)
        before = lax.ppermute(last, axis, up)
        after = lax.ppermute(initial, axis, down)
        x = jnp.concatenate([before, x, after], axis=dim)
    return x


def blend_weights(shift, share, width):
    grid = jnp.arange(width, dtype=jnp.int32)[:, None]
    target = shift + jnp.arange(BOXN, dtype=jnp.int32)[None, :]
    lower = (grid == target).astype(jnp.float32) * (1.0 - share)
    upper = (grid == target + 1).astype(jnp.float32) * share
    return lower + upper


def body(les, tile_owner, tile_slot, box_offset, plane_deficit, plane_box, plane_weight):
    owners = lax.axis_size(("tile", "box"))
    my_index = lax.axis_index(("tile", "box"))
    slab_index = lax.axis_index("slab")
    slab_levels = les.shape[2]
    patch_count = tile_owner.shape[1]
    patch_side = BOXN // TS + 1
    width = patch_side * TS
    box_count = box_offset.shape[0]
    need_count = box_count * patch_count
    slot_count = (need_count + owners - 1) // owners + 1
    sources = tile_owner[:, :, 0].reshape(owners, need_count)
    local_tiles = tile_slot.reshape(owners, need_count)
    from_here = (sources == my_index).astype(jnp.int32)
    slot_rank = jnp.cumsum(from_here, axis=1) - from_here
    slot_ids = jnp.arange(slot_count, dtype=jnp.int32)
    chosen = (from_here[:, None, :] == 1) & (slot_rank[:, None, :] == slot_ids[None, :, None])
    picked = jnp.sum(jnp.where(chosen, local_tiles[:, None, :], 0), axis=2).reshape(-1)
    band_tiles = padded(les, (("slab", 2),), 1)
    outgoing = jnp.take(band_tiles, picked, axis=0)
    incoming = lax.all_to_all(outgoing, ("tile", "box"), split_axis=0, concat_axis=0, tiled=True)
    wanted = lax.dynamic_slice_in_dim(sources, my_index, 1, 0)[0]
    need_ids = jnp.arange(need_count, dtype=jnp.int32)
    same_source = (wanted[:, None] == wanted[None, :]) & (need_ids[None, :] < need_ids[:, None])
    slot_of = jnp.sum(same_source.astype(jnp.int32), axis=1)
    flat_index = (wanted * slot_count + slot_of).reshape(box_count, patch_count)
    slab_points = plane_deficit.shape[1]
    plane_count, contrib_count = plane_box.shape
    deficit_terms = (plane_weight[:, :, None, None] * plane_deficit[:, None, :, :]).reshape(
        plane_count * contrib_count, -1
    )
    box_total = owners * box_count
    onehot = (plane_box.reshape(1, -1) == jnp.arange(box_total, dtype=jnp.int32)[:, None]).astype(
        jnp.float32
    )
    partial_value = jnp.dot(
        onehot, deficit_terms, precision=lax.Precision.HIGHEST, preferred_element_type=jnp.float32
    )
    summed = lax.psum(partial_value, ("tile", "box"))
    wake_loss = lax.dynamic_slice_in_dim(summed, my_index * box_count, box_count, 0)
    wake_loss = wake_loss.reshape(box_count, slab_points, BOXN)
    points = slab_index * slab_points + jnp.arange(slab_points, dtype=jnp.int32)
    level_num = points * (LZ - 1)
    level_low = level_num // (BOXN - 1) - slab_index * slab_levels + 1
    level_frac = (level_num % (BOXN - 1)).astype(jnp.float32) / float(BOXN - 1)
    level_count = incoming.shape[2]
    level_grid = jnp.arange(level_count, dtype=jnp.int32)[:, None]
    height_weights = (level_grid == level_low[None, :]).astype(jnp.float32) * (
        1.0 - level_frac[None, :]
    )
    height_weights = (
        height_weights
        + (level_grid == level_low[None, :] + 1).astype(jnp.float32) * level_frac[None, :]
    )

    def one_box(packed):
        box_ids, offset, box_loss = packed
        patch_tiles = jnp.take(incoming, box_ids, axis=0)
        patch_tiles = patch_tiles.reshape(patch_side, patch_side, 3, level_count, TS, TS)
        share_x = (offset[0] % 8).astype(jnp.float32) / 8.0
        share_y = (offset[1] % 8).astype(jnp.float32) / 8.0
        weights_x = (
            blend_weights(offset[0] // 8, share_x, width)
            .reshape(patch_side, TS, BOXN)
            .astype(jnp.bfloat16)
        )
        weights_y = blend_weights(offset[1] // 8, share_y, width).reshape(patch_side, TS, BOXN)
        along_x = jnp.einsum(
            "rscLyx,sxi->cLryi", patch_tiles, weights_x, preferred_element_type=jnp.float32
        )
        along_y = jnp.einsum(
            "cLryi,ryj->cLji",
            along_x,
            weights_y,
            precision=lax.Precision.HIGHEST,
            preferred_element_type=jnp.float32,
        )
        along_y = along_y.reshape(3, level_count, BOXN * BOXN)
        velocity = jnp.einsum(
            "cLp,Lk->ckp",
            along_y,
            height_weights,
            precision=lax.Precision.HIGHEST,
            preferred_element_type=jnp.float32,
        )
        velocity = velocity.reshape(3, slab_points, BOXN, BOXN)
        velocity = velocity.at[0].add(-box_loss[:, :, None])
        return velocity.astype(jnp.bfloat16).reshape(3, slab_points, BOXN * BOXN)

    box_flow = lax.map(one_box, (flat_index, box_offset, wake_loss))
    extended = padded(box_flow, (("slab", 2),), 1).astype(jnp.float32)
    center = extended[:, :, 1:-1]
    depth = points[None, None, :, None]
    lower_plane = jnp.where(depth == 0, center, extended[:, :, :-2])
    upper_plane = jnp.where(depth == BOXN - 1, center, extended[:, :, 2:])
    column = jnp.arange(BOXN * BOXN, dtype=jnp.int32) % BOXN
    prior_row = jnp.concatenate([center[..., :BOXN], center[..., :-BOXN]], axis=3)
    next_row = jnp.concatenate([center[..., BOXN:], center[..., -BOXN:]], axis=3)
    prior_col = jnp.where(
        column == 0, center, jnp.concatenate([center[..., :1], center[..., :-1]], axis=3)
    )
    next_col = jnp.where(
        column == BOXN - 1, center, jnp.concatenate([center[..., 1:], center[..., -1:]], axis=3)
    )
    stencil_sum = lower_plane - center + (upper_plane - center)
    stencil_sum = stencil_sum + (prior_row - center) + (next_row - center)
    stencil_sum = stencil_sum + (prior_col - center) + (next_col - center)
    return (center + FILTER_NU * stencil_sum).astype(jnp.bfloat16)


def solution(mesh):
    placed = (
        P(("tile", "box"), None, "slab", None),
        P(),
        P(),
        P(("tile", "box"), None),
        P(("tile", "box"), "slab", None),
        P(("tile", "box"), None),
        P(("tile", "box"), None),
    )
    return jax.shard_map(
        body,
        mesh=mesh,
        in_specs=placed,
        out_specs=P(("tile", "box"), None, "slab", None),
        check_vma=False,
    )
```

profile of v0, /device:TPU:0, one launch (start us, length us, event | category | flops | bytes accessed | tf_op | source)
XLA Modules:
  0.0 487.5 jit_solution(6979024093422560494)
XLA Ops:
  6.5 1.7 fusion.74
  9.6 3.0 collective-permute-start
  15.6 3.9 pad_maximum_fusion
  19.4 8.9 %gather_fusion.1 = bf16[144,3,26,256]{3,2,1,0:T(8,128)(2,1)} fusion(bf16[64,3,26,256]{3,2,1,0:T(8,128)(2,1)S(1)} %pad_maximum_fusion, s32[1024]{0:T(1024)S(1)} %pad_clamp_fusion.1), kind=kCustom, calls=%fused_computation.1 | custom fusion | bytes 11502144 | tf_op jit(solution)/shard_map/jit(_take)/gather | solution.py:52
  28.4 6.6 %broadcast_select_fusion.1 = bf16[144,3,26,256]{3,2,1,0:T(8,128)(2,1)} fusion(bf16[144,3,26,256]{3,2,1,0:T(8,128)(2,1)} %gather_fusion.1, pred[144]{0:T(512)(128)(4,1)S(1)} %compare_and_fusion.1), kind=kLoop, calls=%fused_computation.74 | loop fusion | flops 2875392 | bytes 11501712 | tf_op jit(solution)/shard_map/jit(_take)/select_n | solution.py:52
  35.0 8.5 %all-to-all-start = ((bf16[144,3,26,256]{3,2,1,0:T(8,128)(2,1)}), bf16[144,3,26,256]{3,2,1,0:T(8,128)(2,1)}, u32[]{:S(2)}, u32[]{:S(2)}) async-start(bf16[144,3,26,256]{3,2,1,0:T(8,128)(2,1)} %broadcast_select_fusion.1), calls=%async_computation | async-start | bytes 14155776 | tf_op jit(solution)/shard_map/all_to_all | solution.py:53
  45.9 211.5 %all-reduce.2.cloned.1.call-done = f32[80,2048]{1,0:T(8,128)} async-done(((f32[80,2048]{1,0:T(8,128)}), f32[80,2048]{1,0:T(8,128)}) %all-reduce.2.cloned.1.call-update) | async-done | bytes 655376 | tf_op jit(solution)/shard_map/psum | solution.py:71
  258.4 181.3 %while.15 = (s32[]{:T(128)}, bf16[5,3,32,4096]{3,2,1,0:T(8,128)(2,1)}, s32[5,2]{0,1:T(2,128)S(1)}, s32[5,25]{1,0:T(8,128)S(1)}, bf16[144,3,26,256]{3,2,1,0:T(8,1...) while((s32[]{:T(128)}, ...), condition=%wide.region_5.6_spmd.clone, body=%wide.region_4.5_spmd.clone.sunk | while | flops 493983968 | bytes 24612900 | solution.py:122
  264.5 3.6 gather_fusion
  268.1 6.9 %gather.24 = bf16[5,5,3,26,16,16]{5,4,3,2,1,0:T(8,128)(2,1)} reshape(bf16[25,3,26,256]{3,2,1,0:T(8,128)(2,1)S(1)} %gather_fusion) | data formatting | bytes 1996800 | tf_op jit(solution)/shard_map/while/body/eval_jaxpr/jit(_take)/gather | solution.py:90
  275.0 5.6 %fusion.96 = f32[64,5,3,26,16,1]{0,4,5,1,3,2:T(8,128)S(1)} fusion(f32[]{:T(128)S(6)} %div.72, s32[64]{0:T(128)S(1)} %get-tuple-element.283, f32[]{:T(128)S(6)} %sub.148, s32[64]{0:T(128)S(1)} %get-tuple-element.284, s32[5,16]{1,0:T(8,128)S(1)} %multiply_add_fusion.2, bf16[5,5,3,26,16,16]{5,4,3,2,1,0:T(8,128)(2,1)} %gather.24, ...), kind=kOutput, calls=%fused_computation.3.clone.1 | convolution fusion | flops 64427520 | bytes 2596705 | tf_op jit(solution)/shard_map/while/body/eval_jaxpr/rscLyx,sxi->cLryi/dot_general | solution.py:100
  280.6 2.6 fusion.97
  283.2 2.0 reshape.389
  285.3 2.8 convolution_bitcast_fusion.2
  289.0 1.5 reshape.390
  300.7 3.6 gather_fusion
  304.3 6.9 %gather.24 = bf16[5,5,3,26,16,16]{5,4,3,2,1,0:T(8,128)(2,1)} reshape(bf16[25,3,26,256]{3,2,1,0:T(8,128)(2,1)S(1)} %gather_fusion) | data formatting | bytes 1996800 | tf_op jit(solution)/shard_map/while/body/eval_jaxpr/jit(_take)/gather | solution.py:90
  311.2 5.6 %fusion.96 = f32[64,5,3,26,16,1]{0,4,5,1,3,2:T(8,128)S(1)} fusion(f32[]{:T(128)S(6)} %div.72, s32[64]{0:T(128)S(1)} %get-tuple-element.283, f32[]{:T(128)S(6)} %sub.148, s32[64]{0:T(128)S(1)} %get-tuple-element.284, s32[5,16]{1,0:T(8,128)S(1)} %multiply_add_fusion.2, bf16[5,5,3,26,16,16]{5,4,3,2,1,0:T(8,128)(2,1)} %gather.24, ...), kind=kOutput, calls=%fused_computation.3.clone.1 | convolution fusion | flops 64427520 | bytes 2596705 | tf_op jit(solution)/shard_map/while/body/eval_jaxpr/rscLyx,sxi->cLryi/dot_general | solution.py:100
  316.9 2.6 fusion.97
  319.5 2.0 reshape.389
  321.5 2.8 convolution_bitcast_fusion.2
  325.2 1.5 reshape.390
  337.0 3.6 gather_fusion
  340.6 6.9 %gather.24 = bf16[5,5,3,26,16,16]{5,4,3,2,1,0:T(8,128)(2,1)} reshape(bf16[25,3,26,256]{3,2,1,0:T(8,128)(2,1)S(1)} %gather_fusion) | data formatting | bytes 1996800 | tf_op jit(solution)/shard_map/while/body/eval_jaxpr/jit(_take)/gather | solution.py:90
  347.5 5.6 %fusion.96 = f32[64,5,3,26,16,1]{0,4,5,1,3,2:T(8,128)S(1)} fusion(f32[]{:T(128)S(6)} %div.72, s32[64]{0:T(128)S(1)} %get-tuple-element.283, f32[]{:T(128)S(6)} %sub.148, s32[64]{0:T(128)S(1)} %get-tuple-element.284, s32[5,16]{1,0:T(8,128)S(1)} %multiply_add_fusion.2, bf16[5,5,3,26,16,16]{5,4,3,2,1,0:T(8,128)(2,1)} %gather.24, ...), kind=kOutput, calls=%fused_computation.3.clone.1 | convolution fusion | flops 64427520 | bytes 2596705 | tf_op jit(solution)/shard_map/while/body/eval_jaxpr/rscLyx,sxi->cLryi/dot_general | solution.py:100
  353.1 2.6 fusion.97
  355.7 2.0 reshape.389
  357.8 2.8 convolution_bitcast_fusion.2
  361.4 1.5 reshape.390
  373.2 3.6 gather_fusion
  376.8 6.9 %gather.24 = bf16[5,5,3,26,16,16]{5,4,3,2,1,0:T(8,128)(2,1)} reshape(bf16[25,3,26,256]{3,2,1,0:T(8,128)(2,1)S(1)} %gather_fusion) | data formatting | bytes 1996800 | tf_op jit(solution)/shard_map/while/body/eval_jaxpr/jit(_take)/gather | solution.py:90
  383.7 5.6 %fusion.96 = f32[64,5,3,26,16,1]{0,4,5,1,3,2:T(8,128)S(1)} fusion(f32[]{:T(128)S(6)} %div.72, s32[64]{0:T(128)S(1)} %get-tuple-element.283, f32[]{:T(128)S(6)} %sub.148, s32[64]{0:T(128)S(1)} %get-tuple-element.284, s32[5,16]{1,0:T(8,128)S(1)} %multiply_add_fusion.2, bf16[5,5,3,26,16,16]{5,4,3,2,1,0:T(8,128)(2,1)} %gather.24, ...), kind=kOutput, calls=%fused_computation.3.clone.1 | convolution fusion | flops 64427520 | bytes 2596705 | tf_op jit(solution)/shard_map/while/body/eval_jaxpr/rscLyx,sxi->cLryi/dot_general | solution.py:100
  389.3 2.6 fusion.97
  392.0 2.0 reshape.389
  394.0 2.8 convolution_bitcast_fusion.2
  397.7 1.5 reshape.390
  409.4 3.6 gather_fusion
  413.1 6.9 %gather.24 = bf16[5,5,3,26,16,16]{5,4,3,2,1,0:T(8,128)(2,1)} reshape(bf16[25,3,26,256]{3,2,1,0:T(8,128)(2,1)S(1)} %gather_fusion) | data formatting | bytes 1996800 | tf_op jit(solution)/shard_map/while/body/eval_jaxpr/jit(_take)/gather | solution.py:90
  419.9 5.6 %fusion.96 = f32[64,5,3,26,16,1]{0,4,5,1,3,2:T(8,128)S(1)} fusion(f32[]{:T(128)S(6)} %div.72, s32[64]{0:T(128)S(1)} %get-tuple-element.283, f32[]{:T(128)S(6)} %sub.148, s32[64]{0:T(128)S(1)} %get-tuple-element.284, s32[5,16]{1,0:T(8,128)S(1)} %multiply_add_fusion.2, bf16[5,5,3,26,16,16]{5,4,3,2,1,0:T(8,128)(2,1)} %gather.24, ...), kind=kOutput, calls=%fused_computation.3.clone.1 | convolution fusion | flops 64427520 | bytes 2596705 | tf_op jit(solution)/shard_map/while/body/eval_jaxpr/rscLyx,sxi->cLryi/dot_general | solution.py:100
  425.6 2.6 fusion.97
  428.2 2.0 reshape.389
  430.2 2.8 convolution_bitcast_fusion.2
  439.7 4.5 copy.42
  447.1 1.8 collective-permute-done.3
  449.3 1.7 maximum_convert_fusion
  451.1 7.2 %fusion.71 = (f32[5,3,32,4095]{3,2,1,0:T(8,128)}, f32[5,3,32,4095]{3,2,1,0:T(8,128)}) fusion(f32[5,3,34,4096]{3,2,1,0:T(8,128)S(1)} %maximum_convert_fusion), kind=kLoop, calls=%fused_computation.123 | loop fusion | bytes 31449600 | tf_op jit(solution)/shard_map/slice | solution.py:135
  458.3 7.1 %fusion.72 = (f32[5,3,32,4032]{3,2,1,0:T(8,128)}, f32[5,3,32,4032]{3,2,1,0:T(8,128)}) fusion(f32[5,3,34,4096]{3,2,1,0:T(8,128)S(1)} %maximum_convert_fusion), kind=kLoop, calls=%fused_computation.124 | loop fusion | bytes 30965760 | tf_op jit(solution)/shard_map/slice | solution.py:130
  465.4 15.3 %fusion.50 = bf16[5,3,32,4096]{3,2,1,0:T(8,128)(2,1)} fusion(f32[5,3,34,4096]{3,2,1,0:T(8,128)S(1)} %maximum_convert_fusion, f32[5,3,32,4032]{3,2,1,0:T(8,128)} %get-tuple-element.196, f32[5,3,32,64]{3,2,1,0:T(8,128)S(1)} %get-tuple-element.202, f32[5,3,32,64]{3,2,1,0:T(8,128)S(1)} %get-tuple-element.201, f32[5,3,32,4032]{3,2,1,0:T(8,128)} %get-tuple-element.195, ...), kind=kLoop, calls=%fused_computation.71 | loop fusion | flops 43253760 | bytes 58990656 | tf_op jit(solution)/shard_map/convert_element_type | solution.py:140
  (140 shorter events, 41.6 us)
Async XLA Ops:
  8.2 7.0 %collective-permute-start.1 = (bf16[64,3,1,256]{3,0,2,1:T(8,128)(2,1)S(1)}, bf16[64,3,1,256]{3,0,2,1:T(8,128)(2,1)S(1)}, u32[]{:S(2)}, u32[]{:S(2)}) collective-permute-start(bf16[64,3,1,256]{3,0,2,1:T(8,128)(2,1)S(1)} %copy.51), channel_id=1, source_target_pairs={{1,0},{3,2},{5,4},{7,6},{9,8},{11,10},{13,12},{15,14},{17,16},{19,... | collective-permute-start | bytes 294920 | tf_op jit(solution)/shard_map/ppermute | solution.py:20
  9.6 5.8 %collective-permute-start = (bf16[64,3,1,256]{3,0,2,1:T(8,128)(2,1)S(1)}, bf16[64,3,1,256]{3,0,2,1:T(8,128)(2,1)S(1)}, u32[]{:S(2)}, u32[]{:S(2)}) collective-permute-start(bf16[64,3,1,256]{3,0,2,1:T(8,128)(2,1)S(1)} %copy.50), channel_id=1, source_target_pairs={{0,1},{2,3},{4,5},{6,7},{8,9},{10,11},{12,13},{14,15},{16,17},{18,... | collective-permute-start | bytes 294920 | tf_op jit(solution)/shard_map/ppermute | solution.py:19
  35.0 8.8 %copy-start.3 = (s32[4,4]{1,0:T(4,128)S(1)}, s32[4,4]{1,0:T(4,128)}, u32[]{:S(2)}) copy-start(s32[4,4]{1,0:T(4,128)} %param.16) | copy-start | bytes 196
  35.0 8.9 %copy-start.4 = (f32[4,4]{1,0:T(4,128)S(1)}, f32[4,4]{1,0:T(4,128)}, u32[]{:S(2)}) copy-start(f32[4,4]{1,0:T(4,128)} %param.17) | copy-start | bytes 196
  35.0 8.9 %copy-start.1 = (f32[4,32,64]{2,1,0:T(8,128)S(1)}, f32[4,32,64]{2,1,0:T(8,128)}, u32[]{:S(2)}) copy-start(f32[4,32,64]{2,1,0:T(8,128)} %param.15) | copy-start | bytes 98308
  35.0 223.4 %copy-start.2 = (s32[5,2]{0,1:T(2,128)S(1)}, s32[5,2]{0,1:T(2,128)}, u32[]{:S(2)}) copy-start(s32[5,2]{0,1:T(2,128)} %param.14) | copy-start | bytes 124
  35.0 223.4 %all-to-all-start = ((bf16[144,3,26,256]{3,2,1,0:T(8,128)(2,1)}), bf16[144,3,26,256]{3,2,1,0:T(8,128)(2,1)}, u32[]{:S(2)}, u32[]{:S(2)}) async-start(bf16[144,3,26,256]{3,2,1,0:T(8,128)(2,1)} %broadcast_select_fusion.1), calls=%async_computation | async-start | bytes 14155776 | tf_op jit(solution)/shard_map/all_to_all | solution.py:53
  43.5 213.9 %all-reduce.2.cloned.1.call-start = ((), (), s32[]{:S(2)}) async-start(), calls=%async_computation.1 | async-start | bytes 1310720 | tf_op jit(solution)/shard_map/psum | solution.py:71
  439.7 9.4 %copy-start = (bf16[5,3,32,4096]{3,2,1,0:T(8,128)(2,1)S(1)}, bf16[5,3,32,4096]{3,2,1,0:T(8,128)(2,1)}, u32[]{:S(2)}) copy-start(bf16[5,3,32,4096]{3,2,1,0:T(8,128)(2,1)} %get-tuple-element.138) | copy-start | bytes 11796484
  444.2 2.6 collective-permute-start.2
  445.5 3.3 collective-permute-start.3
Sparse Core Ops, SparseCore 0:
  49.7 207.6 all-reduce.1
where the time goes:
time: 489 us; the launch traced here: 488 us
  waiting for transfers between devices  213 us (44%)
  local copies, waits for them, and re-layouts  130 us (27%)
  matrix products  56.9 us (12%)
  other arithmetic  31.4 us (6%)
  loops' own time  26.5 us (5%)
  starting transfers between devices  15.7 us (3%)
  between operations  13.7 us (3%)
    psum x1, waiting for transfers between devices, body(): summed = lax.psum(partial_value, ('tile', 'box'))  212 us
    gather x10, local copies, waits for them, and re-layouts, one_box(): patch_tiles = jnp.take(incoming, box_ids, axis=0)  52.5 us
    dot_general x5, matrix products, one_box(): jnp.einsum('rscLyx,sxi->cLryi', patch_tiles, weights_x, preferred_element...  28.2 us
    another operation x1, loops' own time, body(): box_flow = lax.map(one_box, (flat_index, box_offset, wake_loss))  26.5 us
    convert_element_type x1, other arithmetic, body(): return (center + FILTER_NU * stencil_sum).astype(jnp.bfloat16)  15.3 us
    dot_general x5, matrix products, one_box(): jnp.einsum('cLp,Lk->ckp', along_y, height_weights, precision=lax.Precisio...  14.2 us
    dot_general x5, matrix products, one_box(): jnp.einsum('cLryi,ryj->cLji', along_x, weights_y, precision=lax.Precision...  13.1 us
    another operation x10, local copies, waits for them, and re-layouts  11.5 us
  transfers between devices with their start and end apart: 6, of which 2 were waited for; matrix products, arithmetic and copies ran while one was open for 1% of the time, Pallas kernels for 0%

commit v1 on v0

--- a/solution.py
+++ b/solution.py
@@ -68,7 +68,7 @@
     partial_value = jnp.dot(
         onehot, deficit_terms, precision=lax.Precision.HIGHEST, preferred_element_type=jnp.float32
     )
-    summed = lax.psum(partial_value, ("tile", "box"))
+    summed = jnp.sum(lax.all_gather(partial_value, ("tile", "box")), axis=0)
     wake_loss = lax.dynamic_slice_in_dim(summed, my_index * box_count, box_count, 0)
     wake_loss = wake_loss.reshape(box_count, slab_points, BOXN)
     points = slab_index * slab_points + jnp.arange(slab_points, dtype=jnp.int32)

time: 489 us -> 517 us (1.057)
  waiting for transfers between devices: 213 us -> 235 us
    all_gather x0 -> x1, waiting for transfers between devices: none -> 228 us  [body(): summed = jnp.sum(lax.all_gather(partial_value, ('tile', 'box')), axis=0)]
    psum x1 -> x0, waiting for transfers between devices: 212 us -> none  [body(): summed = lax.psum(partial_value, ('tile', 'box'))]
    all_to_all x1, waiting for transfers between devices: 0.01 us -> 5.66 us  [body(): lax.all_to_all(outgoing, ('tile', 'box'), split_axis=0, concat_axis=0, ti...]
  transfers between devices with their start and end apart: 6 -> 6, of which waited for: 2 -> 3; matrix products, arithmetic and copies ran while one was open for 1% -> 6% of each run, Pallas kernels for 0% -> 0%
where the time goes in v1:
time: 517 us; the launch traced here: 515 us
  waiting for transfers between devices  235 us (45%)
  local copies, waits for them, and re-layouts  131 us (25%)
  matrix products  56.9 us (11%)
  other arithmetic  36.2 us (7%)
  loops' own time  26.1 us (5%)
  starting transfers between devices  15.8 us (3%)
  between operations  13.7 us (3%)
    all_gather x1, waiting for transfers between devices, body(): summed = jnp.sum(lax.all_gather(partial_value, ('tile', 'box')), axis=0)  228 us
    gather x10, local copies, waits for them, and re-layouts, one_box(): patch_tiles = jnp.take(incoming, box_ids, axis=0)  52.4 us
    dot_general x5, matrix products, one_box(): jnp.einsum('rscLyx,sxi->cLryi', patch_tiles, weights_x, preferred_element...  28.2 us
    another operation x1, loops' own time, body(): box_flow = lax.map(one_box, (flat_index, box_offset, wake_loss))  26.1 us
    convert_element_type x1, other arithmetic, body(): return (center + FILTER_NU * stencil_sum).astype(jnp.bfloat16)  15.3 us
    dot_general x5, matrix products, one_box(): jnp.einsum('cLp,Lk->ckp', along_y, height_weights, precision=lax.Precisio...  14.2 us
    dot_general x5, matrix products, one_box(): jnp.einsum('cLryi,ryj->cLji', along_x, weights_y, precision=lax.Precision...  13.1 us
    another operation x10, local copies, waits for them, and re-layouts  11.4 us
  transfers between devices with their start and end apart: 6, of which 3 were waited for; matrix products, arithmetic and copies ran while one was open for 6% of the time, Pallas kernels for 0%

profile of v1, /device:TPU:0, one launch (start us, length us, event | category | flops | bytes accessed | tf_op | source)
XLA Modules:
  0.0 515.2 jit_solution(15751070843197000830)
XLA Ops:
  10.5 1.7 fusion.74
  13.5 3.0 collective-permute-start
  19.5 3.9 pad_maximum_fusion
  23.4 8.9 %gather_fusion.1 = bf16[144,3,26,256]{3,2,1,0:T(8,128)(2,1)} fusion(bf16[64,3,26,256]{3,2,1,0:T(8,128)(2,1)S(1)} %pad_maximum_fusion, s32[1024]{0:T(1024)S(1)} %pad_clamp_fusion.1), kind=kCustom, calls=%fused_computation.1 | custom fusion | bytes 11502144 | tf_op jit(solution)/shard_map/jit(_take)/gather | solution.py:52
  32.3 6.6 %broadcast_select_fusion.1 = bf16[144,3,26,256]{3,2,1,0:T(8,128)(2,1)} fusion(bf16[144,3,26,256]{3,2,1,0:T(8,128)(2,1)} %gather_fusion.1, pred[144]{0:T(512)(128)(4,1)S(1)} %compare_and_fusion.1), kind=kLoop, calls=%fused_computation.74 | loop fusion | flops 2875392 | bytes 11501712 | tf_op jit(solution)/shard_map/jit(_take)/select_n | solution.py:52
  38.9 8.5 %all-to-all-start = ((bf16[144,3,26,256]{3,2,1,0:T(8,128)(2,1)}), bf16[144,3,26,256]{3,2,1,0:T(8,128)(2,1)}, u32[]{:S(2)}, u32[]{:S(2)}) async-start(bf16[144,3,26,256]{3,2,1,0:T(8,128)(2,1)} %broadcast_select_fusion.1), calls=%async_computation | async-start | bytes 14155776 | tf_op jit(solution)/shard_map/all_to_all | solution.py:53
  47.8 228.1 %all-gather.3.cloned.1.call-done = f32[1280,2048]{1,0:T(8,128)} async-done(((f32[80,2048]{1,0:T(8,128)}), f32[1280,2048]{1,0:T(8,128)}) %all-gather.3.cloned.1.call-update) | async-done | bytes 10485776 | tf_op jit(solution)/shard_map/all_gather | solution.py:71
  275.9 4.8 reduce_sum.32
  280.8 5.7 %all-to-all-done = bf16[144,3,26,256]{3,2,1,0:T(8,128)(2,1)} async-done(((bf16[144,3,26,256]{3,2,1,0:T(8,128)(2,1)}), bf16[144,3,26,256]{3,2,1,0:T(8,128)(2,1)}, u32[]{:S(2)}, u32[]{:S(2)}) %all-to-all-start) | async-done | bytes 5750816 | tf_op jit(solution)/shard_map/all_to_all | solution.py:53
  286.4 180.6 %while.15 = (s32[]{:T(128)}, bf16[5,3,32,4096]{3,2,1,0:T(8,128)(2,1)}, s32[5,2]{0,1:T(2,128)S(1)}, s32[5,25]{1,0:T(8,128)S(1)}, bf16[144,3,26,256]{3,2,1,0:T(8,1...) while((s32[]{:T(128)}, ...), condition=%wide.region_5.6_spmd.clone, body=%wide.region_4.5_spmd.clone.sunk | while | flops 493983968 | bytes 24612900 | solution.py:122
  292.4 3.6 gather_fusion
  296.1 6.8 %gather.24 = bf16[5,5,3,26,16,16]{5,4,3,2,1,0:T(8,128)(2,1)} reshape(bf16[25,3,26,256]{3,2,1,0:T(8,128)(2,1)S(1)} %gather_fusion) | data formatting | bytes 1996800 | tf_op jit(solution)/shard_map/while/body/eval_jaxpr/jit(_take)/gather | solution.py:90
  302.9 5.6 %fusion.96 = f32[64,5,3,26,16,1]{0,4,5,1,3,2:T(8,128)S(1)} fusion(f32[]{:T(128)S(6)} %div.72, s32[64]{0:T(128)S(1)} %get-tuple-element.283, f32[]{:T(128)S(6)} %sub.148, s32[64]{0:T(128)S(1)} %get-tuple-element.284, s32[5,16]{1,0:T(8,128)S(1)} %multiply_add_fusion.2, bf16[5,5,3,26,16,16]{5,4,3,2,1,0:T(8,128)(2,1)} %gather.24, ...), kind=kOutput, calls=%fused_computation.3.clone.1 | convolution fusion | flops 64427520 | bytes 2596705 | tf_op jit(solution)/shard_map/while/body/eval_jaxpr/rscLyx,sxi->cLryi/dot_general | solution.py:100
  308.5 2.6 fusion.97
  311.2 2.0 reshape.390
  313.2 2.8 convolution_bitcast_fusion.2
  328.5 3.6 gather_fusion
  332.2 6.8 %gather.24 = bf16[5,5,3,26,16,16]{5,4,3,2,1,0:T(8,128)(2,1)} reshape(bf16[25,3,26,256]{3,2,1,0:T(8,128)(2,1)S(1)} %gather_fusion) | data formatting | bytes 1996800 | tf_op jit(solution)/shard_map/while/body/eval_jaxpr/jit(_take)/gather | solution.py:90
  339.0 5.6 %fusion.96 = f32[64,5,3,26,16,1]{0,4,5,1,3,2:T(8,128)S(1)} fusion(f32[]{:T(128)S(6)} %div.72, s32[64]{0:T(128)S(1)} %get-tuple-element.283, f32[]{:T(128)S(6)} %sub.148, s32[64]{0:T(128)S(1)} %get-tuple-element.284, s32[5,16]{1,0:T(8,128)S(1)} %multiply_add_fusion.2, bf16[5,5,3,26,16,16]{5,4,3,2,1,0:T(8,128)(2,1)} %gather.24, ...), kind=kOutput, calls=%fused_computation.3.clone.1 | convolution fusion | flops 64427520 | bytes 2596705 | tf_op jit(solution)/shard_map/while/body/eval_jaxpr/rscLyx,sxi->cLryi/dot_general | solution.py:100
  344.7 2.6 fusion.97
  347.3 2.0 reshape.390
  349.3 2.8 convolution_bitcast_fusion.2
  353.0 1.5 reshape.391
  364.7 3.6 gather_fusion
  368.3 6.8 %gather.24 = bf16[5,5,3,26,16,16]{5,4,3,2,1,0:T(8,128)(2,1)} reshape(bf16[25,3,26,256]{3,2,1,0:T(8,128)(2,1)S(1)} %gather_fusion) | data formatting | bytes 1996800 | tf_op jit(solution)/shard_map/while/body/eval_jaxpr/jit(_take)/gather | solution.py:90
  375.1 5.6 %fusion.96 = f32[64,5,3,26,16,1]{0,4,5,1,3,2:T(8,128)S(1)} fusion(f32[]{:T(128)S(6)} %div.72, s32[64]{0:T(128)S(1)} %get-tuple-element.283, f32[]{:T(128)S(6)} %sub.148, s32[64]{0:T(128)S(1)} %get-tuple-element.284, s32[5,16]{1,0:T(8,128)S(1)} %multiply_add_fusion.2, bf16[5,5,3,26,16,16]{5,4,3,2,1,0:T(8,128)(2,1)} %gather.24, ...), kind=kOutput, calls=%fused_computation.3.clone.1 | convolution fusion | flops 64427520 | bytes 2596705 | tf_op jit(solution)/shard_map/while/body/eval_jaxpr/rscLyx,sxi->cLryi/dot_general | solution.py:100
  380.8 2.6 fusion.97
  383.4 2.0 reshape.390
  385.4 2.8 convolution_bitcast_fusion.2
  400.8 3.6 gather_fusion
  404.4 6.8 %gather.24 = bf16[5,5,3,26,16,16]{5,4,3,2,1,0:T(8,128)(2,1)} reshape(bf16[25,3,26,256]{3,2,1,0:T(8,128)(2,1)S(1)} %gather_fusion) | data formatting | bytes 1996800 | tf_op jit(solution)/shard_map/while/body/eval_jaxpr/jit(_take)/gather | solution.py:90
  411.3 5.6 %fusion.96 = f32[64,5,3,26,16,1]{0,4,5,1,3,2:T(8,128)S(1)} fusion(f32[]{:T(128)S(6)} %div.72, s32[64]{0:T(128)S(1)} %get-tuple-element.283, f32[]{:T(128)S(6)} %sub.148, s32[64]{0:T(128)S(1)} %get-tuple-element.284, s32[5,16]{1,0:T(8,128)S(1)} %multiply_add_fusion.2, bf16[5,5,3,26,16,16]{5,4,3,2,1,0:T(8,128)(2,1)} %gather.24, ...), kind=kOutput, calls=%fused_computation.3.clone.1 | convolution fusion | flops 64427520 | bytes 2596705 | tf_op jit(solution)/shard_map/while/body/eval_jaxpr/rscLyx,sxi->cLryi/dot_general | solution.py:100
  416.9 2.6 fusion.97
  419.5 2.0 reshape.390
  421.5 2.8 convolution_bitcast_fusion.2
  436.9 3.6 gather_fusion
  440.5 6.8 %gather.24 = bf16[5,5,3,26,16,16]{5,4,3,2,1,0:T(8,128)(2,1)} reshape(bf16[25,3,26,256]{3,2,1,0:T(8,128)(2,1)S(1)} %gather_fusion) | data formatting | bytes 1996800 | tf_op jit(solution)/shard_map/while/body/eval_jaxpr/jit(_take)/gather | solution.py:90
  447.4 5.6 %fusion.96 = f32[64,5,3,26,16,1]{0,4,5,1,3,2:T(8,128)S(1)} fusion(f32[]{:T(128)S(6)} %div.72, s32[64]{0:T(128)S(1)} %get-tuple-element.283, f32[]{:T(128)S(6)} %sub.148, s32[64]{0:T(128)S(1)} %get-tuple-element.284, s32[5,16]{1,0:T(8,128)S(1)} %multiply_add_fusion.2, bf16[5,5,3,26,16,16]{5,4,3,2,1,0:T(8,128)(2,1)} %gather.24, ...), kind=kOutput, calls=%fused_computation.3.clone.1 | convolution fusion | flops 64427520 | bytes 2596705 | tf_op jit(solution)/shard_map/while/body/eval_jaxpr/rscLyx,sxi->cLryi/dot_general | solution.py:100
  453.0 2.6 fusion.97
  455.7 2.0 reshape.390
  457.6 2.8 convolution_bitcast_fusion.2
  467.1 4.5 copy.42
  471.6 1.7 collective-permute-start.2
  474.8 1.8 collective-permute-done.3
  477.1 1.7 maximum_convert_fusion
  478.8 7.1 %fusion.71 = (f32[5,3,32,4095]{3,2,1,0:T(8,128)}, f32[5,3,32,4095]{3,2,1,0:T(8,128)}) fusion(f32[5,3,34,4096]{3,2,1,0:T(8,128)S(1)} %maximum_convert_fusion), kind=kLoop, calls=%fused_computation.123 | loop fusion | bytes 31449600 | tf_op jit(solution)/shard_map/slice | solution.py:135
  485.9 7.1 %fusion.72 = (f32[5,3,32,4032]{3,2,1,0:T(8,128)}, f32[5,3,32,4032]{3,2,1,0:T(8,128)}) fusion(f32[5,3,34,4096]{3,2,1,0:T(8,128)S(1)} %maximum_convert_fusion), kind=kLoop, calls=%fused_computation.124 | loop fusion | bytes 30965760 | tf_op jit(solution)/shard_map/slice | solution.py:130
  493.0 15.3 %fusion.50 = bf16[5,3,32,4096]{3,2,1,0:T(8,128)(2,1)} fusion(f32[5,3,34,4096]{3,2,1,0:T(8,128)S(1)} %maximum_convert_fusion, f32[5,3,32,4032]{3,2,1,0:T(8,128)} %get-tuple-element.196, f32[5,3,32,64]{3,2,1,0:T(8,128)S(1)} %get-tuple-element.202, f32[5,3,32,64]{3,2,1,0:T(8,128)S(1)} %get-tuple-element.201, f32[5,3,32,4032]{3,2,1,0:T(8,128)} %get-tuple-element.195, ...), kind=kLoop, calls=%fused_computation.71 | loop fusion | flops 43253760 | bytes 58990656 | tf_op jit(solution)/shard_map/convert_element_type | solution.py:140
  (135 shorter events, 45.8 us)
Async XLA Ops:
  6.5 269.3 %all-gather.3.cloned.1.call-start = ((), (), s32[]{:S(2)}) async-start(), calls=%async_computation.1 | async-start | bytes 11141120 | tf_op jit(solution)/shard_map/all_gather | solution.py:71
  12.2 7.0 %collective-permute-start.1 = (bf16[64,3,1,256]{3,0,2,1:T(8,128)(2,1)S(1)}, bf16[64,3,1,256]{3,0,2,1:T(8,128)(2,1)S(1)}, u32[]{:S(2)}, u32[]{:S(2)}) collective-permute-start(bf16[64,3,1,256]{3,0,2,1:T(8,128)(2,1)S(1)} %copy.51), channel_id=1, source_target_pairs={{1,0},{3,2},{5,4},{7,6},{9,8},{11,10},{13,12},{15,14},{17,16},{19,... | collective-permute-start | bytes 294920 | tf_op jit(solution)/shard_map/ppermute | solution.py:20
  13.5 5.8 %collective-permute-start = (bf16[64,3,1,256]{3,0,2,1:T(8,128)(2,1)S(1)}, bf16[64,3,1,256]{3,0,2,1:T(8,128)(2,1)S(1)}, u32[]{:S(2)}, u32[]{:S(2)}) collective-permute-start(bf16[64,3,1,256]{3,0,2,1:T(8,128)(2,1)S(1)} %copy.50), channel_id=1, source_target_pairs={{0,1},{2,3},{4,5},{6,7},{8,9},{10,11},{12,13},{14,15},{16,17},{18,... | collective-permute-start | bytes 294920 | tf_op jit(solution)/shard_map/ppermute | solution.py:19
  38.9 247.6 %all-to-all-start = ((bf16[144,3,26,256]{3,2,1,0:T(8,128)(2,1)}), bf16[144,3,26,256]{3,2,1,0:T(8,128)(2,1)}, u32[]{:S(2)}, u32[]{:S(2)}) async-start(bf16[144,3,26,256]{3,2,1,0:T(8,128)(2,1)} %broadcast_select_fusion.1), calls=%async_computation | async-start | bytes 14155776 | tf_op jit(solution)/shard_map/all_to_all | solution.py:53
  47.4 239.1 %copy-start.1 = (s32[5,2]{0,1:T(2,128)S(1)}, s32[5,2]{0,1:T(2,128)}, u32[]{:S(2)}) copy-start(s32[5,2]{0,1:T(2,128)} %param.14) | copy-start | bytes 124
  467.1 9.8 %copy-start = (bf16[5,3,32,4096]{3,2,1,0:T(8,128)(2,1)S(1)}, bf16[5,3,32,4096]{3,2,1,0:T(8,128)(2,1)}, u32[]{:S(2)}) copy-start(bf16[5,3,32,4096]{3,2,1,0:T(8,128)(2,1)} %get-tuple-element.138) | copy-start | bytes 11796484
  471.6 3.0 collective-permute-start.2
  473.2 3.3 collective-permute-start.3
Sparse Core Ops, SparseCore 0:
  10.6 265.2 all-gather.2
